TPU v7x, 32 devices: a whole 2x2x4 slice. The times are simulated.
32 devices in a mesh: gx: 2 (over y), gy: 4 (over x, core), gz: 4 (over z).
Axes of the slice: x: 2, y: 2, z: 4, core: 2. Of those that a mesh axis runs over, the one named last changes fastest.
Arguments:
- block_state: bfloat16 [2, 64, 10, 32, 1024], P('gx', ('gy', 'gz')), may hold values from -6 to 6
- block_level: int32 [2, 64], P('gx'), may hold values from 0 to 2, as said below
- block_velocity: bfloat16 [2, 64, 3], P('gx', ('gy', 'gz')), may hold values from -1 to 1
- diffusivity: float32 [10], replicated, may hold values from 0.05 to 0.6
- reaction_matrix: float32 [10, 10], replicated, may hold values from -3 to 3
- ghost_source: int32 [2, 64, 6], P('gx'), may hold values from 0 to 63, as said below
- swap_bit: int32 [2, 4, 4], P('gx', 'gy', 'gz'), may hold values from -1 to 0, as said below
- swap_slot: int32 [2, 4, 4], P('gx', 'gy', 'gz'), may hold values from 0 to 3, as said below
Outputs:
- new_state: bfloat16 [2, 64, 10, 32, 1024], P('gx', ('gy', 'gz'))
Inputs may be any that keep to these rules, and one draw needn't show every extreme that they name: `block_level`: levels are 0, 1 or 2; all blocks of some devices have level 2. `ghost_source`: ghost sources lie in the same gx slab; blocks of a slab are numbered device by device in gy+gz order, 4 a device. Among the 24 ghost faces of the blocks of one device, at most 2 come from the blocks of any one device, and exactly 2 from some device. `swap_bit`: all devices of one (gy, gz) column share the value, so trade partners are paired; -1 means that the column trades no block. `swap_slot`: of two partners, the one whose sum of 2 ** level over its blocks is larger (ties: the lower gx index) names its first block of highest level, the other its first block of lowest level.
All inputs are finite; a program needn't handle non-finite values.
Results may differ from a plain program's by a relative error of at most 0.001.
Values may be sent and summed in bfloat16 or wider, within the bound.
A program may use at most 128 MiB of HBM per device.

v0:
```python
import functools

import jax
import jax.numpy as jnp
from jax import lax
from jax.experimental import pallas as pl
from jax.experimental.pallas import tpu as pltpu
from jax.sharding import PartitionSpec as P

dt_base = 0.05
VMEM_LIMIT = 56 * 1024 * 1024


def swapped(x, axis, bit):
    return lax.ppermute(x, axis, [(i, i ^ 1 << bit) for i in range(lax.axis_size(axis))])


def lane_iota():
    return lax.broadcasted_iota(jnp.int32, (8, 128), 1)


def row_iota():
    return lax.broadcasted_iota(jnp.int32, (8, 128), 0)


def regroup_matrix():
    r = lax.broadcasted_iota(jnp.int32, (512, 512), 0)
    c = lax.broadcasted_iota(jnp.int32, (512, 512), 1)
    target = (r // 32) % 4 * 128 + r // 128 * 32 + r % 32
    return jnp.where(c == target, 1.0, 0.0).astype(jnp.bfloat16)


def regroup_in(x_ref, matrix, rows):
    fields = x_ref.shape[1]
    height = fields * 32
    for half in range(2):
        tiles = [
            x_ref[0, :, :, 128 * (half + 2 * m) : 128 * (half + 2 * m) + 128].reshape(height, 128)
            for m in range(4)
        ]
        moved = jnp.dot(
            jnp.concatenate(tiles, axis=1), matrix[...], preferred_element_type=jnp.float32
        )
        for g in range(4):
            at = (half * 4 + g) * height
            rows[at : at + height, :] = moved[:, 128 * g : 128 * g + 128]


def plane_rows(fields, f, ii, jj):
    return pl.ds(jj * fields * 32 + f * 32 + ii, 8, stride=4)


def pack_kernel(sel_ref, x_ref, out_ref, faces, rows, matrix):
    step = pl.program_id(0)
    fields = x_ref.shape[1]
    lane = lane_iota()
    k = lane % 32

    @pl.when(step == 0)
    def _():
        matrix[...] = regroup_matrix()

    regroup_in(x_ref, matrix, rows)

    def pair(fp, carry):
        got = [[], [], [], [], [], []]
        for half in range(2):
            f = fp * 2 + half
            got[0].append(rows[pl.ds(f * 32, 8, stride=fields * 32), :])
            got[1].append(rows[pl.ds(f * 32 + 31, 8, stride=fields * 32), :])
            low_y = high_y = low_z = high_z = jnp.zeros((8, 128), jnp.float32)
            for ii in range(4):
                for jj in range(8):
                    plane = rows[plane_rows(fields, f, ii, jj), :]
                    n = ii * 8 + jj
                    here = k == n
                    low_z = jnp.where(here, pltpu.roll(plane, n, 1) if n else plane, low_z)
                    high_z = jnp.where(
                        here, pltpu.roll(plane, n + 97, 1) if n != 31 else plane, high_z
                    )
                    here = lane // 32 == ii
                    if jj == 0:
                        low_y = jnp.where(here, pltpu.roll(plane, 32 * ii, 1) if ii else plane, low_y)
                    if jj == 7:
                        moved = pltpu.roll(plane, 32 * ii + 32, 1) if ii != 3 else plane
                        high_y = jnp.where(here, moved, high_y)
            got[2].append(low_y)
            got[3].append(high_y)
            got[4].append(low_z)
            got[5].append(high_z)
        at = pl.multiple_of(fp * 16, 16)
        for face in range(6):
            both = jnp.concatenate(got[face], axis=0).astype(jnp.bfloat16)
            faces[step * 6 + face, pl.ds(at, 16), :] = both
        return carry

    lax.fori_loop(0, fields // 2, pair, 0)

    @pl.when(step == pl.num_programs(0) - 1)
    def _():
        def place(n, carry):
            out_ref[n] = faces[sel_ref[n]]
            return carry

        lax.fori_loop(0, out_ref.shape[0], place, 0, unroll=4)


def pack_faces(blocks, sel):
    per_dev, fields, cells, plane = blocks.shape
    return pl.pallas_call(
        pack_kernel,
        grid_spec=pltpu.PrefetchScalarGridSpec(
            num_scalar_prefetch=1,
            grid=(per_dev,),
            in_specs=[pl.BlockSpec((1, fields, cells, plane), lambda g, *_: (g, 0, 0, 0))],
            out_specs=pl.BlockSpec((sel.shape[0], fields * 8, 128), lambda g, *_: (0, 0, 0)),
            scratch_shapes=[
                pltpu.VMEM((per_dev * 6, fields * 8, 128), jnp.bfloat16),
                pltpu.VMEM((fields * 256, 128), jnp.float32),
                pltpu.VMEM((512, 512), jnp.bfloat16),
            ],
        ),
        out_shape=jax.ShapeDtypeStruct((sel.shape[0], fields * 8, 128), jnp.bfloat16),
        compiler_params=pltpu.CompilerParams(vmem_limit_bytes=VMEM_LIMIT),
    )(sel, blocks)


def pair_sum(x, distance, axis, bit_clear):
    size = x.shape[axis]
    other = jnp.where(
        bit_clear, pltpu.roll(x, size - distance, axis), pltpu.roll(x, distance, axis)
    )
    return x + other


def advance_kernel(
    meta_ref, speed_ref, rate_ref, react_ref,
    x_ref, faces_ref, o_ref,
    u, ghost, layers, ends, coef, rows, matrix,
):
    fields = x_ref.shape[1]
    step = pl.program_id(0)
    count = pl.num_programs(0)
    per_dev = speed_ref.shape[0] // 3
    requests = per_dev * 6
    block = meta_ref[step]
    own_level = meta_ref[per_dev + block]
    substeps = jnp.left_shift(jnp.int32(1), own_level)
    scale = substeps.astype(jnp.float32)
    dt = jnp.where(own_level == 0, dt_base, jnp.where(own_level == 1, dt_base / 2, dt_base / 4))
    lane, row = lane_iota(), row_iota()
    k = lane % 32
    at_low_z, at_high_z = k == 0, k == 31

    @pl.when(step == 0)
    def _():
        matrix[...] = regroup_matrix()

    regroup_in(x_ref, matrix, rows)

    tall_lane = lax.broadcasted_iota(jnp.int32, (fields * 8, 128), 1)
    tall_row = lax.broadcasted_iota(jnp.int32, (fields * 8, 128), 0)
    for face in range(6):
        request = block * 6 + face
        layers[face] = faces_ref[meta_ref[2 * per_dev + request]].astype(jnp.float32)

        @pl.when(meta_ref[2 * per_dev + requests + request] > 0)
        def _():
            v = pair_sum(layers[face], 1, 1, tall_lane % 2 == 0)
            if face < 2:
                v = pair_sum(v, 1, 0, tall_row % 2 == 0)
            elif face < 4:
                v = pair_sum(v, 32, 1, tall_lane // 32 % 2 == 0)
            else:
                v = pair_sum(v, 8, 1, tall_lane // 8 % 2 == 0)
            layers[face] = v * 0.25

    speeds = [speed_ref[block * 3 + d] for d in range(3)]
    minus = [jnp.maximum(v, 0.0) * scale * dt for v in speeds]
    plus = [-jnp.minimum(v, 0.0) * scale * dt for v in speeds]
    outflow = minus[0] + plus[0] + minus[1] + plus[1] + minus[2] + plus[2]

    def halo_low_x(plane, f, jj):
        edge = layers[0, pl.ds(f * 8 + jj, 1), :]
        return jnp.where(row == 0, edge, pltpu.roll(plane, 1, 0))

    def halo_high_x(plane, f, jj):
        edge = layers[1, pl.ds(f * 8 + jj, 1), :]
        return jnp.where(row == 7, edge, pltpu.roll(plane, 7, 0))

    def halo_low_y(plane, f, ii):
        return jnp.where(lane < 32, ends[0, f, ii], pltpu.roll(plane, 32, 1))

    def halo_high_y(plane, f, ii):
        return jnp.where(lane >= 96, ends[1, f, ii], pltpu.roll(plane, 96, 1))

    def prepare(f, carry):
        rate = rate_ref[f] * (scale * scale) * dt
        coef[f, 0] = jnp.full((8, 128), rate + minus[0])
        coef[f, 1] = jnp.full((8, 128), rate + plus[0])
        coef[f, 2] = jnp.full((8, 128), rate + minus[1])
        coef[f, 3] = jnp.full((8, 128), rate + plus[1])
        coef[f, 4] = jnp.where(at_low_z, 0.0, rate + minus[2])
        coef[f, 5] = jnp.where(at_high_z, 0.0, rate + plus[2])
        for e in range(fields):
            own = jnp.where(f == e, 1.0 - 6.0 * rate - outflow, 0.0)
            coef[f, 6 + e] = jnp.full((8, 128), dt * react_ref[f * fields + e] + own)

        at = pl.ds(pl.multiple_of(f * 8, 8), 8)
        low_y, high_y = layers[2, at, :], layers[3, at, :]
        low_z = layers[4, at, :] * (rate + minus[2])
        high_z = layers[5, at, :] * (rate + plus[2])
        for ii in range(4):
            ends[0, f, ii] = pltpu.roll(low_y, 128 - 32 * ii, 1) if ii else low_y
            ends[1, f, ii] = pltpu.roll(high_y, 96 - 32 * ii, 1) if ii != 3 else high_y
        for ii in range(4):
            for jj in range(8):
                n = ii * 8 + jj
                low = pltpu.roll(low_z, 128 - n, 1) if n else low_z
                high = pltpu.roll(high_z, 31 - n, 1) if n != 31 else high_z
                ghost[f, ii, jj] = jnp.where(at_low_z, low, jnp.where(at_high_z, high, 0.0))
                plane = rows[plane_rows(fields, f, ii, jj), :]
                u[0, f, ii + 1, jj + 1] = plane
                if ii == 0:
                    u[0, f, 5, jj + 1] = halo_high_x(plane, f, jj)
                if ii == 3:
                    u[0, f, 0, jj + 1] = halo_low_x(plane, f, jj)
                if jj == 0:
                    u[0, f, ii + 1, 9] = halo_high_y(plane, f, ii)
                if jj == 7:
                    u[0, f, ii + 1, 0] = halo_low_y(plane, f, ii)
        return carry

    lax.fori_loop(0, fields, prepare, 0)

    def substep(index, carry):
        now = index % 2
        later = 1 - now

        def planes(jj, inner):
            mid = [[u[now, f, ii + 1, jj + 1] for ii in range(4)] for f in range(fields)]
            for f in range(fields):
                before = [u[now, f, 0, jj + 1]] + mid[f][:-1]
                after = mid[f][1:] + [u[now, f, 5, jj + 1]]
                total = []
                for ii in range(4):
                    c = mid[f][ii]
                    v = ghost[f, ii, jj] + coef[f, 0] * before[ii]
                    v = v + coef[f, 1] * after[ii]
                    v = v + coef[f, 2] * u[now, f, ii + 1, jj]
                    v = v + coef[f, 3] * u[now, f, ii + 1, jj + 2]
                    v = v + coef[f, 4] * pltpu.roll(c, 1, 1)
                    v = v + coef[f, 5] * pltpu.roll(c, 127, 1)
                    total.append(v)
                for e in range(fields):
                    weight = coef[f, 6 + e]
                    for ii in range(4):
                        total[ii] = total[ii] + weight * mid[e][ii]
                for ii in range(4):
                    u[later, f, ii + 1, jj + 1] = total[ii]
                u[later, f, 5, jj + 1] = halo_high_x(total[0], f, jj)
                u[later, f, 0, jj + 1] = halo_low_x(total[3], f, jj)
            return inner

        lax.fori_loop(0, 8, planes, 0)

        def halos(f, inner):
            for ii in range(4):
                u[later, f, ii + 1, 9] = halo_high_y(u[later, f, ii + 1, 1], f, ii)
                u[later, f, ii + 1, 0] = halo_low_y(u[later, f, ii + 1, 8], f, ii)
            return inner

        lax.fori_loop(0, fields, halos, 0, unroll=5)
        return carry

    lax.fori_loop(0, substeps, substep, 0)
    last = substeps % 2
    height = fields * 32

    def finish(f, carry):
        for ii in range(4):
            for jj in range(8):
                rows[plane_rows(fields, f, ii, jj), :] = u[last, f, ii + 1, jj + 1]
        return carry

    lax.fori_loop(0, fields, finish, 0)
    for half in range(2):
        tiles = []
        for g in range(4):
            at = (half * 4 + g) * height
            tiles.append(rows[at : at + height, :].astype(jnp.bfloat16))
        moved = jnp.dot(
            jnp.concatenate(tiles, axis=1), matrix[...], preferred_element_type=jnp.float32
        ).astype(jnp.bfloat16)
        for m in range(4):
            at = 128 * (half + 2 * m)
            o_ref[0, :, :, at : at + 128] = moved[:, 128 * m : 128 * m + 128].reshape(
                fields, 32, 128
            )


def advance(blocks, faces, meta, count, scalars, out_blocks):
    per_dev, fields, cells, plane = blocks.shape
    block_shape = (1, fields, cells, plane)
    picked = lambda g, meta, *_: (meta[g], 0, 0, 0)
    return pl.pallas_call(
        advance_kernel,
        grid_spec=pltpu.PrefetchScalarGridSpec(
            num_scalar_prefetch=4,
            grid=(count,),
            in_specs=[
                pl.BlockSpec(block_shape, picked),
                pl.BlockSpec(faces.shape, lambda g, *_: (0, 0, 0)),
            ],
            out_specs=pl.BlockSpec(
                block_shape, picked if out_blocks > 1 else lambda g, *_: (0, 0, 0, 0)
            ),
            scratch_shapes=[
                pltpu.VMEM((2, fields, 6, 10, 8, 128), jnp.float32),
                pltpu.VMEM((fields, 4, 8, 8, 128), jnp.float32),
                pltpu.VMEM((6, fields * 8, 128), jnp.float32),
                pltpu.VMEM((2, fields, 4, 8, 128), jnp.float32),
                pltpu.VMEM((fields, 6 + fields, 8, 128), jnp.float32),
                pltpu.VMEM((fields * 256, 128), jnp.float32),
                pltpu.VMEM((512, 512), jnp.bfloat16),
            ],
        ),
        out_shape=jax.ShapeDtypeStruct((out_blocks, fields, cells, plane), jnp.bfloat16),
        compiler_params=pltpu.CompilerParams(vmem_limit_bytes=VMEM_LIMIT),
        cost_estimate=pl.CostEstimate(
            flops=count * 40_000_000_000, bytes_accessed=count * 1_400_000, transcendentals=0
        ),
    )(meta, *scalars, blocks, faces)


def local(
    block_state,
    block_level,
    block_velocity,
    diffusivity,
    reaction_matrix,
    ghost_source,
    swap_bit,
    swap_slot,
):
    blocks = block_state[0]
    per_dev = blocks.shape[0]
    requests = per_dev * 6
    peers = lax.axis_size(("gy", "gz"))
    my_index = lax.axis_index(("gy", "gz"))
    base = my_index * per_dev
    wanted = ghost_source[0].reshape(peers, requests)
    order = jnp.arange(requests, dtype=jnp.int32)[None, :]
    code = order * 64 + wanted % per_dev * 6 + (order % 6 ^ 1)
    match = wanted // per_dev == my_index
    first = jnp.min(jnp.where(match, code, requests * 64), axis=1)
    final = jnp.max(jnp.where(match, code, 0), axis=1)
    sel = jnp.stack([first, final], axis=1).reshape(2 * peers) % 64

    outgoing = pack_faces(blocks, sel)
    arrived = lax.all_to_all(outgoing, ("gy", "gz"), split_axis=0, concat_axis=0, tiled=True)

    slot_here = swap_slot[0, 0, 0]
    bit_here = swap_bit[0, 0, 0]
    levels = block_level[0]
    mine = lax.dynamic_index_in_dim(wanted, my_index, 0, keepdims=False)
    source_dev = mine // per_dev
    earlier = jnp.arange(requests)[None, :] < jnp.arange(requests)[:, None]
    second = jnp.any((source_dev[:, None] == source_dev[None, :]) & earlier, axis=1)
    lookup = source_dev * 2 + second.astype(jnp.int32)
    own_levels = lax.dynamic_slice_in_dim(levels, base, per_dev, 0)
    numbers = jnp.arange(levels.shape[0], dtype=jnp.int32)
    donor_levels = jnp.sum(
        jnp.where(mine[:, None] == numbers[None, :], levels[None, :], 0), axis=1
    )
    differs = (donor_levels != jnp.repeat(own_levels, 6)).astype(jnp.int32)
    others = jnp.arange(per_dev, dtype=jnp.int32)
    others = (others + (others >= slot_here).astype(jnp.int32)) % per_dev
    tail = jnp.concatenate([own_levels, lookup, differs])
    meta_first = jnp.concatenate([jnp.full((per_dev,), slot_here), tail])
    meta_rest = jnp.concatenate([others, tail])
    scalars = (
        block_velocity[0].astype(jnp.float32).reshape(-1),
        diffusivity,
        reaction_matrix.reshape(-1),
    )
    departing = advance(blocks, arrived, meta_first, 1, scalars, 1)
    bit_count = lax.axis_size("gx").bit_length() - 1
    partners = [swapped(departing, "gx", bit_no) for bit_no in range(bit_count)]
    rest = advance(blocks, arrived, meta_rest, per_dev - 1, scalars, per_dev)
    coming = departing
    for bit_no in range(bit_count):
        coming = jnp.where(bit_here == bit_no, partners[bit_no], coming)
    result = lax.dynamic_update_index_in_dim(rest, coming[0], slot_here, 0)
    return result[None]


def solution(mesh):
    in_specs = (
        P("gx", ("gy", "gz"), None, None, None),
        P("gx", None),
        P("gx", ("gy", "gz"), None),
        P(),
        P(),
        P("gx", None, None),
        P("gx", "gy", "gz"),
        P("gx", "gy", "gz"),
    )
    out_specs = P("gx", ("gy", "gz"), None, None, None)
    return jax.shard_map(local, mesh=mesh, in_specs=in_specs, out_specs=out_specs, check_vma=False)
```

profile of v0, /device:TPU:1, one launch (start us, length us, event | category | flops | bytes accessed | tf_op | source)
XLA Modules:
  0.0 97.4 jit_solution(16519567278243650592)
XLA Ops:
  0.0 0.0 copy-start.2
  0.0 0.0 copy-start.4
  0.0 0.0 copy-start.3
  0.0 0.0 copy-start.5
  0.1 0.1 add.98
  0.2 0.1 add.93
  0.3 0.7 select_reduce_fusion.2
  1.0 0.1 reduce_min.14
  1.1 0.1 reduce_max.14
  1.1 0.1 reduce_min.18
  1.3 0.1 reduce_max.18
  1.4 0.1 copy.21
  1.5 0.1 reshape.94
  1.6 0.6 and_select_fusion.sel_ref
  2.2 7.9 %shard_map.82 = bf16[32,80,128]{2,1,0:T(8,128)(2,1)} custom-call(s32[32]{0:T(128)} %and_select_fusion.sel_ref, bf16[4,10,32,1024]{3,2,1,0:T(8,128)(2,1)} %bitcast.25), custom_call_target="tpu_custom_call" | custom-call | tf_op jit(solution)/shard_map/pallas_call | solution.py:110
  10.1 7.3 %all-to-all-start = ((bf16[32,80,128]{2,1,0:T(8,128)(2,1)}), bf16[32,80,128]{2,1,0:T(8,128)(2,1)S(1)}, u32[]{:S(2)}, u32[]{:S(2)}) async-start(bf16[32,80,128]{2,1,0:T(8,128)(2,1)} %shard_map.82), calls=%async_computation | async-start | bytes 1310720 | tf_op jit(solution)/shard_map/all_to_all | solution.py:361
  17.4 0.0 copy-done.2
  17.4 0.1 copy.16
  18.8 0.0 copy-done.4
  18.8 0.6 reshape.95.speed_ref
  19.4 0.0 copy-done.3
  19.4 0.7 reshape.93.react_ref
  20.1 0.0 copy-done.5
  20.1 0.1 fusion.15
  20.2 0.1 broadcast_in_dim.40
  20.2 0.1 reshape.92
  20.3 0.1 reshape_squeeze.3
  20.4 0.2 select_reduce_fusion
  20.6 0.2 fusion.1
  20.8 0.6 add_add_fusion.1
  21.5 13.7 %all-to-all-done.faces_ref = bf16[32,80,128]{2,1,0:T(8,128)(2,1)S(1)} async-done(((bf16[32,80,128]{2,1,0:T(8,128)(2,1)}), bf16[32,80,128]{2,1,0:T(8,128)(2,1)S(1)}, u32[]{:S(2)}, u32[]{:S(2)}) %all-to-all-start) | async-done | bytes 655392 | tf_op jit(solution)/shard_map/all_to_all | solution.py:361
  35.2 0.0 copy-start.1
  35.2 0.8 copy-done.1
  36.0 16.6 %shard_map.84 = bf16[1,10,32,1024]{3,2,1,0:T(8,128)(2,1)} custom-call(s32[56]{0:T(128)} %get-tuple-element.9.meta_ref, f32[12]{0:T(128)} %reshape.95.speed_ref, f32[10]{0:T(128)} %rate_ref.3, f32[100]{0:T(128)} %reshape.93.react_ref, bf16[4,10,32,1024]{3,2,1,0:T(8,128)(2,1)} %bitcast.26, bf16[32,80,128]{2,1,0:T(8,128)(2,1)} %copy-done.1), custom_call_target="tpu_custom_call" | custom-call | flops 40000000000 | bytes 1400000 | tf_op jit(solution)/shard_map/pallas_call | solution.py:306
  52.6 0.0 collective-permute-start
  52.6 0.0 copy-start
  52.6 43.6 %shard_map.83 = bf16[4,10,32,1024]{3,2,1,0:T(8,128)(2,1)} custom-call(s32[56]{0:T(128)} %get-tuple-element.10.meta_ref, f32[12]{0:T(128)} %reshape.95.speed_ref, f32[10]{0:T(128)} %rate_ref.3, f32[100]{0:T(128)} %reshape.93.react_ref, bf16[4,10,32,1024]{3,2,1,0:T(8,128)(2,1)} %bitcast.27, bf16[32,80,128]{2,1,0:T(8,128)(2,1)} %copy-done.1), custom_call_target="tpu_custom_call" | custom-call | flops 120000004096 | bytes 4200000 | tf_op jit(solution)/shard_map/pallas_call | solution.py:306
  96.2 0.0 collective-permute-done
  96.2 0.0 copy-done
  96.3 1.1 %bitcast_dynamic-update-slice_fusion = bf16[1,4,10,32,1024]{4,3,2,1,0:T(8,128)(2,1)} fusion(bf16[1,4,10,32,1024]{4,3,2,1,0:T(8,128)(2,1)} %bitcast.30, s32[]{:T(128)S(6)} %select_n.97, bf16[1,10,32,1024]{3,2,1,0:T(8,128)(2,1)S(1)} %collective-permute-done, bf16[1,10,32,1024]{3,2,1,0:T(8,128)(2,1)S(1)} %copy-done, pred[]{:T(512)} %bitcast.9), kind=kLoop, calls=%fused_computation | loop fusion | flops 327680 | bytes 1966596 | tf_op jit(solution)/shard_map/jit(dynamic_update_index_in_dim)/dynamic_update_slice | solution.py:394
  (11 shorter events, 0.1 us)
Async XLA Ops:
  0.0 17.4 %copy-start.2 = (s32[1,64,6]{1,0,2:T(1,128)S(1)}, s32[1,64,6]{1,0,2:T(1,128)}, u32[]{:S(2)}) copy-start(s32[1,64,6]{1,0,2:T(1,128)} %param.13) | copy-start | bytes 4612
  0.0 18.8 %copy-start.4 = (bf16[1,4,3]{2,1,0:T(4,128)(2,1)S(1)}, bf16[1,4,3]{2,1,0:T(4,128)(2,1)}, u32[]{:S(2)}) copy-start(bf16[1,4,3]{2,1,0:T(4,128)(2,1)} %param.10) | copy-start | bytes 76
  0.0 19.4 %copy-start.3 = (f32[10,10]{1,0:T(8,128)S(1)}, f32[10,10]{1,0:T(8,128)}, u32[]{:S(2)}) copy-start(f32[10,10]{1,0:T(8,128)} %param.12) | copy-start | bytes 1204
  0.0 20.1 %copy-start.5 = (s32[1,64]{1,0:T(1,128)S(1)}, s32[1,64]{1,0:T(1,128)}, u32[]{:S(2)}) copy-start(s32[1,64]{1,0:T(1,128)} %param.9) | copy-start | bytes 772
  10.1 25.1 %all-to-all-start = ((bf16[32,80,128]{2,1,0:T(8,128)(2,1)}), bf16[32,80,128]{2,1,0:T(8,128)(2,1)S(1)}, u32[]{:S(2)}, u32[]{:S(2)}) async-start(bf16[32,80,128]{2,1,0:T(8,128)(2,1)} %shard_map.82), calls=%async_computation | async-start | bytes 1310720 | tf_op jit(solution)/shard_map/all_to_all | solution.py:361
  35.2 0.8 copy-start.1
  52.6 43.6 %collective-permute-start = (bf16[1,10,32,1024]{3,2,1,0:T(8,128)(2,1)}, bf16[1,10,32,1024]{3,2,1,0:T(8,128)(2,1)S(1)}, u32[]{:S(2)}, u32[]{:S(2)}) collective-permute-start(bf16[1,10,32,1024]{3,2,1,0:T(8,128)(2,1)} %shard_map.84), channel_id=1, source_target_pairs={{0,16},{16,0},{1,17},{17,1},{2,18},{18,2},{3,19},{19,3},{4,20},{20... | collective-permute-start | bytes 1966088 | tf_op jit(solution)/shard_map/ppermute | solution.py:15
  52.6 43.6 %copy-start = (bf16[1,10,32,1024]{3,2,1,0:T(8,128)(2,1)S(1)}, bf16[1,10,32,1024]{3,2,1,0:T(8,128)(2,1)}, u32[]{:S(2)}) copy-start(bf16[1,10,32,1024]{3,2,1,0:T(8,128)(2,1)} %shard_map.84) | copy-start | bytes 1966084
where the time goes:
time: 98.2 us; the launch traced here: 97.4 us
  Pallas kernels  68.1 us (69%)
  waiting for transfers between devices  13.7 us (14%)
  starting transfers between devices  7.33 us (7%)
  other arithmetic  3.74 us (4%)
  local copies, waits for them, and re-layouts  3.04 us (3%)
  between operations  1.43 us (1%)
    pallas_call x2, Pallas kernels, advance(): pl.pallas_call(advance_kernel, grid_spec=pltpu.PrefetchScalarGridSpec(num...  60.2 us
    all_to_all x1, waiting for transfers between devices, local(): lax.all_to_all(outgoing, ('gy', 'gz'), split_axis=0, concat_axis=0, tiled...  13.7 us
    pallas_call x1, Pallas kernels, pack_faces(): pl.pallas_call(pack_kernel, grid_spec=pltpu.PrefetchScalarGridSpec(num_sc...  7.87 us
    all_to_all x1, starting transfers between devices, local(): lax.all_to_all(outgoing, ('gy', 'gz'), split_axis=0, concat_axis=0, tiled...  7.32 us
  transfers between devices with their start and end apart: 2, of which 1 were waited for; matrix products, arithmetic and copies ran while one was open for 3% of the time, Pallas kernels for 45%

commit v1 on v0

--- a/solution.py
+++ b/solution.py
@@ -88,13 +88,14 @@
             got[3].append(high_y)
             got[4].append(low_z)
             got[5].append(high_z)
-        at = pl.multiple_of(fp * 16, 16)
+        at = fp * 16
         for face in range(6):
             both = jnp.concatenate(got[face], axis=0).astype(jnp.bfloat16)
             faces[step * 6 + face, pl.ds(at, 16), :] = both
         return carry
 
-    lax.fori_loop(0, fields // 2, pair, 0)
+    for fp in range(fields // 2):
+        pair(fp, 0)
 
     @pl.when(step == pl.num_programs(0) - 1)
     def _():
@@ -134,9 +135,9 @@
 
 
 def advance_kernel(
-    meta_ref, speed_ref, rate_ref, react_ref,
-    x_ref, faces_ref, o_ref,
-    u, ghost, layers, ends, coef, rows, matrix,
+    meta_ref, speed_ref, rate_ref,
+    react_ref, centre_ref, x_ref, faces_ref, o_ref,
+    u, ghost, layers, ends, coef, mixer, rows, matrix,
 ):
     fields = x_ref.shape[1]
     step = pl.program_id(0)
@@ -202,9 +203,6 @@
         coef[f, 3] = jnp.full((8, 128), rate + plus[1])
         coef[f, 4] = jnp.where(at_low_z, 0.0, rate + minus[2])
         coef[f, 5] = jnp.where(at_high_z, 0.0, rate + plus[2])
-        for e in range(fields):
-            own = jnp.where(f == e, 1.0 - 6.0 * rate - outflow, 0.0)
-            coef[f, 6 + e] = jnp.full((8, 128), dt * react_ref[f * fields + e] + own)
 
         at = pl.ds(pl.multiple_of(f * 8, 8), 8)
         low_y, high_y = layers[2, at, :], layers[3, at, :]
@@ -231,38 +229,55 @@
                     u[0, f, ii + 1, 0] = halo_low_y(plane, f, ii)
         return carry
 
-    lax.fori_loop(0, fields, prepare, 0)
+    lax.fori_loop(0, fields, prepare, 0, unroll=2)
+
+    height8 = fields * 8
+    wide_row = lax.broadcasted_iota(jnp.int32, (height8, 3 * height8), 0)
+    wide_lane = lax.broadcasted_iota(jnp.int32, (height8, 3 * height8), 1)
+    own = jnp.where(wide_lane % height8 == wide_row, 1.0 - outflow, 0.0)
+    mix = react_ref[...] * dt + own - centre_ref[...] * (6.0 * scale * scale * dt)
+    mix_high = mix.astype(jnp.bfloat16)
+    mix_low = (mix - mix_high.astype(jnp.float32)).astype(jnp.bfloat16)
+    mixer[...] = jnp.where(wide_lane < 2 * height8, mix_high, mix_low)
 
     def substep(index, carry):
         now = index % 2
         later = 1 - now
 
         def planes(jj, inner):
-            mid = [[u[now, f, ii + 1, jj + 1] for ii in range(4)] for f in range(fields)]
+            columns = []
+            for ii in range(4):
+                value = jnp.concatenate(
+                    [u[now, f, ii + 1, jj + 1] for f in range(fields)], axis=0
+                )
+                high = value.astype(jnp.bfloat16)
+                low = (value - high.astype(jnp.float32)).astype(jnp.bfloat16)
+                columns.append(jnp.concatenate([high, low, high], axis=0))
+            mixed = jnp.dot(
+                mixer[...], jnp.concatenate(columns, axis=1), preferred_element_type=jnp.float32
+            )
             for f in range(fields):
-                before = [u[now, f, 0, jj + 1]] + mid[f][:-1]
-                after = mid[f][1:] + [u[now, f, 5, jj + 1]]
+                mid = [u[now, f, ii + 1, jj + 1] for ii in range(4)]
+                before = [u[now, f, 0, jj + 1]] + mid[:-1]
+                after = mid[1:] + [u[now, f, 5, jj + 1]]
                 total = []
                 for ii in range(4):
-                    c = mid[f][ii]
-                    v = ghost[f, ii, jj] + coef[f, 0] * before[ii]
+                    c = mid[ii]
+                    v = mixed[8 * f : 8 * f + 8, 128 * ii : 128 * ii + 128] + ghost[f, ii, jj]
+                    v = v + coef[f, 0] * before[ii]
                     v = v + coef[f, 1] * after[ii]
                     v = v + coef[f, 2] * u[now, f, ii + 1, jj]
                     v = v + coef[f, 3] * u[now, f, ii + 1, jj + 2]
                     v = v + coef[f, 4] * pltpu.roll(c, 1, 1)
                     v = v + coef[f, 5] * pltpu.roll(c, 127, 1)
                     total.append(v)
-                for e in range(fields):
-                    weight = coef[f, 6 + e]
-                    for ii in range(4):
-                        total[ii] = total[ii] + weight * mid[e][ii]
                 for ii in range(4):
                     u[later, f, ii + 1, jj + 1] = total[ii]
                 u[later, f, 5, jj + 1] = halo_high_x(total[0], f, jj)
                 u[later, f, 0, jj + 1] = halo_low_x(total[3], f, jj)
             return inner
 
-        lax.fori_loop(0, 8, planes, 0)
+        lax.fori_loop(0, 8, planes, 0, unroll=2)
 
         def halos(f, inner):
             for ii in range(4):
@@ -306,9 +321,11 @@
     return pl.pallas_call(
         advance_kernel,
         grid_spec=pltpu.PrefetchScalarGridSpec(
-            num_scalar_prefetch=4,
+            num_scalar_prefetch=3,
             grid=(count,),
             in_specs=[
+                pl.BlockSpec((fields * 8, fields * 24), lambda g, *_: (0, 0)),
+                pl.BlockSpec((fields * 8, fields * 24), lambda g, *_: (0, 0)),
                 pl.BlockSpec(block_shape, picked),
                 pl.BlockSpec(faces.shape, lambda g, *_: (0, 0, 0)),
             ],
@@ -320,7 +337,8 @@
                 pltpu.VMEM((fields, 4, 8, 8, 128), jnp.float32),
                 pltpu.VMEM((6, fields * 8, 128), jnp.float32),
                 pltpu.VMEM((2, fields, 4, 8, 128), jnp.float32),
-                pltpu.VMEM((fields, 6 + fields, 8, 128), jnp.float32),
+                pltpu.VMEM((fields, 6, 8, 128), jnp.float32),
+                pltpu.VMEM((fields * 8, fields * 24), jnp.bfloat16),
                 pltpu.VMEM((fields * 256, 128), jnp.float32),
                 pltpu.VMEM((512, 512), jnp.bfloat16),
             ],
@@ -382,7 +400,8 @@
     scalars = (
         block_velocity[0].astype(jnp.float32).reshape(-1),
         diffusivity,
-        reaction_matrix.reshape(-1),
+        jnp.tile(jnp.kron(reaction_matrix, jnp.eye(8)), (1, 3)),
+        jnp.tile(jnp.diag(jnp.repeat(diffusivity, 8)), (1, 3)),
     )
     departing = advance(blocks, arrived, meta_first, 1, scalars, 1)
     bit_count = lax.axis_size("gx").bit_length() - 1

time: 98.2 us -> 166 us (1.69)
  the two profiles are of different devices: /device:TPU:1 before, /device:TPU:8 now
where the time goes in v1:
time: 166 us
  Pallas kernels  137 us (83%)
  waiting for transfers between devices  10.7 us (6%)
  starting transfers between devices  7.71 us (5%)
  local copies, waits for them, and re-layouts  4.33 us (3%)
  other arithmetic  3.91 us (2%)
    pallas_call x2, Pallas kernels, advance(): pl.pallas_call(advance_kernel, grid_spec=pltpu.PrefetchScalarGridSpec(num...  131 us
    all_to_all x1, waiting for transfers between devices, local(): lax.all_to_all(outgoing, ('gy', 'gz'), split_axis=0, concat_axis=0, tiled...  10.7 us
    pallas_call x1, Pallas kernels, pack_faces(): pl.pallas_call(pack_kernel, grid_spec=pltpu.PrefetchScalarGridSpec(num_sc...  6.53 us
    all_to_all x1, starting transfers between devices, local(): lax.all_to_all(outgoing, ('gy', 'gz'), split_axis=0, concat_axis=0, tiled...  6.27 us
  transfers between devices with their start and end apart: 2, of which 1 were waited for; matrix products, arithmetic and copies ran while one was open for 3% of the time, Pallas kernels for 58%

profile of v1, /device:TPU:8, one launch (start us, length us, event | category | flops | bytes accessed | tf_op | source)
XLA Modules:
  0.0 165.5 jit_solution(9855609725116731675)
XLA Ops:
  0.0 0.0 copy-start.2
  0.0 0.0 copy-start.5
  0.0 0.0 copy-start.4
  0.0 0.0 copy-start.3
  0.1 0.1 add.98
  0.2 0.1 add.93
  0.3 0.7 select_reduce_fusion.2
  1.0 0.1 reduce_min.14
  1.1 0.1 reduce_max.14
  1.1 0.1 reduce_min.18
  1.3 0.1 reduce_max.18
  1.4 0.1 copy.27
  1.5 0.1 reshape.146
  1.6 0.6 and_select_fusion.sel_ref
  2.2 0.0 copy-start.6
  2.2 6.5 %shard_map.82 = bf16[32,80,128]{2,1,0:T(8,128)(2,1)} custom-call(s32[32]{0:T(128)} %and_select_fusion.sel_ref, bf16[4,10,32,1024]{3,2,1,0:T(8,128)(2,1)} %bitcast.27), custom_call_target="tpu_custom_call" | custom-call | tf_op jit(solution)/shard_map/pallas_call | solution.py:111
  8.7 6.3 %all-to-all-start = ((bf16[32,80,128]{2,1,0:T(8,128)(2,1)}), bf16[32,80,128]{2,1,0:T(8,128)(2,1)S(1)}, u32[]{:S(2)}, u32[]{:S(2)}) async-start(bf16[32,80,128]{2,1,0:T(8,128)(2,1)} %shard_map.82), calls=%async_computation | async-start | bytes 1310720 | tf_op jit(solution)/shard_map/all_to_all | solution.py:379
  15.0 0.0 copy-done.2
  15.0 0.1 copy.21
  16.4 0.0 copy-done.5
  16.4 0.7 reshape.147.speed_ref
  17.1 0.0 copy-done.4
  17.1 0.1 broadcast_in_dim.68
  17.2 0.1 broadcast_in_dim.69
  17.2 0.0 copy-done.3
  17.3 0.1 broadcast_multiply_fusion
  17.4 0.0 copy-done.6
  17.4 0.1 fusion.17
  17.5 0.1 broadcast_in_dim.67
  17.5 0.1 reshape.145
  17.6 0.1 reshape_squeeze.3
  17.7 0.7 copy.29.centre_ref
  18.4 0.2 mul.58
  18.6 0.1 copy.22
  18.7 0.7 copy.28.react_ref
  19.5 0.2 select_reduce_fusion
  19.7 0.2 fusion.2
  19.9 0.7 add_add_fusion.1
  20.6 10.7 %all-to-all-done.faces_ref = bf16[32,80,128]{2,1,0:T(8,128)(2,1)S(1)} async-done(((bf16[32,80,128]{2,1,0:T(8,128)(2,1)}), bf16[32,80,128]{2,1,0:T(8,128)(2,1)S(1)}, u32[]{:S(2)}, u32[]{:S(2)}) %all-to-all-start) | async-done | bytes 655392 | tf_op jit(solution)/shard_map/all_to_all | solution.py:379
  31.3 0.0 copy-start.1
  31.3 0.8 copy-done.1
  32.1 34.2 %shard_map.84 = bf16[1,10,32,1024]{3,2,1,0:T(8,128)(2,1)} custom-call(s32[56]{0:T(128)} %get-tuple-element.9.meta_ref, f32[12]{0:T(128)} %reshape.147.speed_ref, f32[10]{0:T(128)} %rate_ref.3, f32[80,240]{1,0:T(8,128)} %copy.28.react_ref, f32[80,240]{1,0:T(8,128)} %copy.29.centre_ref, bf16[4,10,32,1024]{3,2,1,0:T(8,128)(2,1)} %bitcast.28, ...), custom_call_target="tpu_custom_call" | custom-call | flops 40000000000 | bytes 1400000 | tf_op jit(solution)/shard_map/pallas_call | solution.py:321
  66.3 1.4 collective-permute-start
  67.8 0.0 copy-start
  67.8 96.7 %shard_map.83 = bf16[4,10,32,1024]{3,2,1,0:T(8,128)(2,1)} custom-call(s32[56]{0:T(128)} %get-tuple-element.10.meta_ref, f32[12]{0:T(128)} %reshape.147.speed_ref, f32[10]{0:T(128)} %rate_ref.3, f32[80,240]{1,0:T(8,128)} %copy.28.react_ref, f32[80,240]{1,0:T(8,128)} %copy.29.centre_ref, bf16[4,10,32,1024]{3,2,1,0:T(8,128)(2,1)} %bitcast.29, ...), custom_call_target="tpu_custom_call" | custom-call | flops 120000004096 | bytes 4200000 | tf_op jit(solution)/shard_map/pallas_call | solution.py:321
  164.4 0.0 collective-permute-done
  164.4 0.0 copy-done
  164.4 1.1 bitcast_dynamic-update-slice_fusion
  (15 shorter events, 0.1 us)
Async XLA Ops:
  0.0 15.0 %copy-start.2 = (s32[1,64,6]{1,0,2:T(1,128)S(1)}, s32[1,64,6]{1,0,2:T(1,128)}, u32[]{:S(2)}) copy-start(s32[1,64,6]{1,0,2:T(1,128)} %param.13) | copy-start | bytes 4612
  0.0 16.4 %copy-start.5 = (bf16[1,4,3]{2,1,0:T(4,128)(2,1)S(1)}, bf16[1,4,3]{2,1,0:T(4,128)(2,1)}, u32[]{:S(2)}) copy-start(bf16[1,4,3]{2,1,0:T(4,128)(2,1)} %param.10) | copy-start | bytes 76
  0.0 17.1 %copy-start.4 = (f32[10]{0:T(128)S(1)}, f32[10]{0:T(128)}, u32[]{:S(2)}) copy-start(f32[10]{0:T(128)} %rate_ref.3) | copy-start | bytes 124
  0.0 17.2 %copy-start.3 = (f32[10,10]{1,0:T(8,128)S(1)}, f32[10,10]{1,0:T(8,128)}, u32[]{:S(2)}) copy-start(f32[10,10]{1,0:T(8,128)} %param.12) | copy-start | bytes 1204
  2.2 15.2 %copy-start.6 = (s32[1,64]{1,0:T(1,128)S(1)}, s32[1,64]{1,0:T(1,128)}, u32[]{:S(2)}) copy-start(s32[1,64]{1,0:T(1,128)} %param.9) | copy-start | bytes 772
  8.7 22.5 %all-to-all-start = ((bf16[32,80,128]{2,1,0:T(8,128)(2,1)}), bf16[32,80,128]{2,1,0:T(8,128)(2,1)S(1)}, u32[]{:S(2)}, u32[]{:S(2)}) async-start(bf16[32,80,128]{2,1,0:T(8,128)(2,1)} %shard_map.82), calls=%async_computation | async-start | bytes 1310720 | tf_op jit(solution)/shard_map/all_to_all | solution.py:379
  31.3 0.8 copy-start.1
  66.3 98.1 %collective-permute-start = (bf16[1,10,32,1024]{3,2,1,0:T(8,128)(2,1)}, bf16[1,10,32,1024]{3,2,1,0:T(8,128)(2,1)S(1)}, u32[]{:S(2)}, u32[]{:S(2)}) collective-permute-start(bf16[1,10,32,1024]{3,2,1,0:T(8,128)(2,1)} %shard_map.84), channel_id=1, source_target_pairs={{0,16},{16,0},{1,17},{17,1},{2,18},{18,2},{3,19},{19,3},{4,20},{20... | collective-permute-start | bytes 1966088 | tf_op jit(solution)/shard_map/ppermute | solution.py:15
  67.8 96.7 %copy-start = (bf16[1,10,32,1024]{3,2,1,0:T(8,128)(2,1)S(1)}, bf16[1,10,32,1024]{3,2,1,0:T(8,128)(2,1)}, u32[]{:S(2)}) copy-start(bf16[1,10,32,1024]{3,2,1,0:T(8,128)(2,1)} %shard_map.84) | copy-start | bytes 1966084

commit v2 on v0

--- a/solution.py
+++ b/solution.py
@@ -23,55 +23,51 @@
     return lax.broadcasted_iota(jnp.int32, (8, 128), 0)
 
 
-def regroup_matrix():
-    r = lax.broadcasted_iota(jnp.int32, (512, 512), 0)
-    c = lax.broadcasted_iota(jnp.int32, (512, 512), 1)
-    target = (r // 32) % 4 * 128 + r // 128 * 32 + r % 32
-    return jnp.where(c == target, 1.0, 0.0).astype(jnp.bfloat16)
-
-
-def regroup_in(x_ref, matrix, rows):
-    fields = x_ref.shape[1]
-    height = fields * 32
+def exchange_groups(tiles):
+    group = lax.broadcasted_iota(jnp.int32, tiles[0].shape, 1) // 32
+    odd, upper = group % 2 == 1, group >= 2
+    stage = [None] * 4
+    for m in (0, 2):
+        stage[m] = jnp.where(odd, pltpu.roll(tiles[m + 1], 32, 1), tiles[m])
+        stage[m + 1] = jnp.where(odd, tiles[m + 1], pltpu.roll(tiles[m], 96, 1))
+    done = [None] * 4
+    for m in (0, 1):
+        done[m] = jnp.where(upper, pltpu.roll(stage[m + 2], 64, 1), stage[m])
+        done[m + 2] = jnp.where(upper, stage[m + 2], pltpu.roll(stage[m], 64, 1))
+    return done
+
+
+def regroup_in(x_ref, f, rows):
     for half in range(2):
-        tiles = [
-            x_ref[0, :, :, 128 * (half + 2 * m) : 128 * (half + 2 * m) + 128].reshape(height, 128)
-            for m in range(4)
-        ]
-        moved = jnp.dot(
-            jnp.concatenate(tiles, axis=1), matrix[...], preferred_element_type=jnp.float32
-        )
-        for g in range(4):
-            at = (half * 4 + g) * height
-            rows[at : at + height, :] = moved[:, 128 * g : 128 * g + 128]
-
-
-def plane_rows(fields, f, ii, jj):
-    return pl.ds(jj * fields * 32 + f * 32 + ii, 8, stride=4)
-
-
-def pack_kernel(sel_ref, x_ref, out_ref, faces, rows, matrix):
+        tiles = []
+        for m in range(4):
+            at = 128 * (half + 2 * m)
+            tiles.append(x_ref[0, f, :, at : at + 128].astype(jnp.float32))
+        for g, tile in enumerate(exchange_groups(tiles)):
+            rows[pl.ds(f * 256 + (half * 4 + g) * 32, 32), :] = tile
+
+
+def plane_rows(f, ii, jj):
+    return pl.ds(f * 256 + jj * 32 + ii, 8, stride=4)
+
+
+def pack_kernel(sel_ref, x_ref, out_ref, faces, rows):
     step = pl.program_id(0)
     fields = x_ref.shape[1]
     lane = lane_iota()
     k = lane % 32
 
-    @pl.when(step == 0)
-    def _():
-        matrix[...] = regroup_matrix()
-
-    regroup_in(x_ref, matrix, rows)
-
     def pair(fp, carry):
         got = [[], [], [], [], [], []]
         for half in range(2):
             f = fp * 2 + half
-            got[0].append(rows[pl.ds(f * 32, 8, stride=fields * 32), :])
-            got[1].append(rows[pl.ds(f * 32 + 31, 8, stride=fields * 32), :])
+            regroup_in(x_ref, f, rows)
+            got[0].append(rows[pl.ds(f * 256, 8, stride=32), :])
+            got[1].append(rows[pl.ds(f * 256 + 31, 8, stride=32), :])
             low_y = high_y = low_z = high_z = jnp.zeros((8, 128), jnp.float32)
             for ii in range(4):
                 for jj in range(8):
-                    plane = rows[plane_rows(fields, f, ii, jj), :]
+                    plane = rows[plane_rows(f, ii, jj), :]
                     n = ii * 8 + jj
                     here = k == n
                     low_z = jnp.where(here, pltpu.roll(plane, n, 1) if n else plane, low_z)
@@ -88,13 +84,14 @@
             got[3].append(high_y)
             got[4].append(low_z)
             got[5].append(high_z)
-        at = pl.multiple_of(fp * 16, 16)
+        at = fp * 16
         for face in range(6):
             both = jnp.concatenate(got[face], axis=0).astype(jnp.bfloat16)
             faces[step * 6 + face, pl.ds(at, 16), :] = both
         return carry
 
-    lax.fori_loop(0, fields // 2, pair, 0)
+    for fp in range(fields // 2):
+        pair(fp, 0)
 
     @pl.when(step == pl.num_programs(0) - 1)
     def _():
@@ -117,7 +114,6 @@
             scratch_shapes=[
                 pltpu.VMEM((per_dev * 6, fields * 8, 128), jnp.bfloat16),
                 pltpu.VMEM((fields * 256, 128), jnp.float32),
-                pltpu.VMEM((512, 512), jnp.bfloat16),
             ],
         ),
         out_shape=jax.ShapeDtypeStruct((sel.shape[0], fields * 8, 128), jnp.bfloat16),
@@ -136,11 +132,10 @@
 def advance_kernel(
     meta_ref, speed_ref, rate_ref, react_ref,
     x_ref, faces_ref, o_ref,
-    u, ghost, layers, ends, coef, rows, matrix,
+    u, ghost, layers, ends, coef, rows,
 ):
     fields = x_ref.shape[1]
     step = pl.program_id(0)
-    count = pl.num_programs(0)
     per_dev = speed_ref.shape[0] // 3
     requests = per_dev * 6
     block = meta_ref[step]
@@ -152,12 +147,6 @@
     k = lane % 32
     at_low_z, at_high_z = k == 0, k == 31
 
-    @pl.when(step == 0)
-    def _():
-        matrix[...] = regroup_matrix()
-
-    regroup_in(x_ref, matrix, rows)
-
     tall_lane = lax.broadcasted_iota(jnp.int32, (fields * 8, 128), 1)
     tall_row = lax.broadcasted_iota(jnp.int32, (fields * 8, 128), 0)
     for face in range(6):
@@ -195,6 +184,7 @@
         return jnp.where(lane >= 96, ends[1, f, ii], pltpu.roll(plane, 96, 1))
 
     def prepare(f, carry):
+        regroup_in(x_ref, f, rows)
         rate = rate_ref[f] * (scale * scale) * dt
         coef[f, 0] = jnp.full((8, 128), rate + minus[0])
         coef[f, 1] = jnp.full((8, 128), rate + plus[0])
@@ -219,7 +209,7 @@
                 low = pltpu.roll(low_z, 128 - n, 1) if n else low_z
                 high = pltpu.roll(high_z, 31 - n, 1) if n != 31 else high_z
                 ghost[f, ii, jj] = jnp.where(at_low_z, low, jnp.where(at_high_z, high, 0.0))
-                plane = rows[plane_rows(fields, f, ii, jj), :]
+                plane = rows[plane_rows(f, ii, jj), :]
                 u[0, f, ii + 1, jj + 1] = plane
                 if ii == 0:
                     u[0, f, 5, jj + 1] = halo_high_x(plane, f, jj)
@@ -231,7 +221,7 @@
                     u[0, f, ii + 1, 0] = halo_low_y(plane, f, ii)
         return carry
 
-    lax.fori_loop(0, fields, prepare, 0)
+    lax.fori_loop(0, fields, prepare, 0, unroll=2)
 
     def substep(index, carry):
         now = index % 2
@@ -262,7 +252,7 @@
                 u[later, f, 0, jj + 1] = halo_low_x(total[3], f, jj)
             return inner
 
-        lax.fori_loop(0, 8, planes, 0)
+        lax.fori_loop(0, 8, planes, 0, unroll=2)
 
         def halos(f, inner):
             for ii in range(4):
@@ -275,28 +265,19 @@
 
     lax.fori_loop(0, substeps, substep, 0)
     last = substeps % 2
-    height = fields * 32
 
     def finish(f, carry):
         for ii in range(4):
             for jj in range(8):
-                rows[plane_rows(fields, f, ii, jj), :] = u[last, f, ii + 1, jj + 1]
+                rows[plane_rows(f, ii, jj), :] = u[last, f, ii + 1, jj + 1]
+        for half in range(2):
+            tiles = [rows[pl.ds(f * 256 + (half * 4 + g) * 32, 32), :] for g in range(4)]
+            for m, tile in enumerate(exchange_groups(tiles)):
+                at = 128 * (half + 2 * m)
+                o_ref[0, f, :, at : at + 128] = tile.astype(jnp.bfloat16)
         return carry
 
-    lax.fori_loop(0, fields, finish, 0)
-    for half in range(2):
-        tiles = []
-        for g in range(4):
-            at = (half * 4 + g) * height
-            tiles.append(rows[at : at + height, :].astype(jnp.bfloat16))
-        moved = jnp.dot(
-            jnp.concatenate(tiles, axis=1), matrix[...], preferred_element_type=jnp.float32
-        ).astype(jnp.bfloat16)
-        for m in range(4):
-            at = 128 * (half + 2 * m)
-            o_ref[0, :, :, at : at + 128] = moved[:, 128 * m : 128 * m + 128].reshape(
-                fields, 32, 128
-            )
+    lax.fori_loop(0, fields, finish, 0, unroll=2)
 
 
 def advance(blocks, faces, meta, count, scalars, out_blocks):
@@ -322,7 +303,6 @@
                 pltpu.VMEM((2, fields, 4, 8, 128), jnp.float32),
                 pltpu.VMEM((fields, 6 + fields, 8, 128), jnp.float32),
                 pltpu.VMEM((fields * 256, 128), jnp.float32),
-                pltpu.VMEM((512, 512), jnp.bfloat16),
             ],
         ),
         out_shape=jax.ShapeDtypeStruct((out_blocks, fields, cells, plane), jnp.bfloat16),

time: 98.2 us -> 105 us (1.069)
  the two profiles are of different devices: /device:TPU:1 before, /device:TPU:8 now
where the time goes in v2:
time: 105 us; the launch traced here: 104 us
  Pallas kernels  75.9 us (72%)
  waiting for transfers between devices  12.2 us (12%)
  starting transfers between devices  7.95 us (8%)
  other arithmetic  3.74 us (4%)
  local copies, waits for them, and re-layouts  3.04 us (3%)
  between operations  1.43 us (1%)
    pallas_call x2, Pallas kernels, advance(): pl.pallas_call(advance_kernel, grid_spec=pltpu.PrefetchScalarGridSpec(num...  62.3 us
    pallas_call x1, Pallas kernels, pack_faces(): pl.pallas_call(pack_kernel, grid_spec=pltpu.PrefetchScalarGridSpec(num_sc...  13.6 us
    all_to_all x1, waiting for transfers between devices, local(): lax.all_to_all(outgoing, ('gy', 'gz'), split_axis=0, concat_axis=0, tiled...  12.2 us
    all_to_all x1, starting transfers between devices, local(): lax.all_to_all(outgoing, ('gy', 'gz'), split_axis=0, concat_axis=0, tiled...  6.27 us
  transfers between devices with their start and end apart: 2, of which 1 were waited for; matrix products, arithmetic and copies ran while one was open for 3% of the time, Pallas kernels for 44%

profile of v2, /device:TPU:8, one launch (start us, length us, event | category | flops | bytes accessed | tf_op | source)
XLA Modules:
  0.0 104.3 jit_solution(7300132304849440303)
XLA Ops:
  0.0 0.0 copy-start.2
  0.0 0.0 copy-start.4
  0.0 0.0 copy-start.3
  0.0 0.0 copy-start.5
  0.1 0.1 add.98
  0.2 0.1 add.93
  0.3 0.7 select_reduce_fusion.2
  1.0 0.1 reduce_min.14
  1.1 0.1 reduce_max.14
  1.1 0.1 reduce_min.18
  1.3 0.1 reduce_max.18
  1.4 0.1 copy.21
  1.5 0.1 reshape.94
  1.6 0.6 and_select_fusion.sel_ref
  2.2 13.6 %shard_map.82 = bf16[32,80,128]{2,1,0:T(8,128)(2,1)} custom-call(s32[32]{0:T(128)} %and_select_fusion.sel_ref, bf16[4,10,32,1024]{3,2,1,0:T(8,128)(2,1)} %bitcast.25), custom_call_target="tpu_custom_call" | custom-call | tf_op jit(solution)/shard_map/pallas_call | solution.py:107
  15.8 6.3 %all-to-all-start = ((bf16[32,80,128]{2,1,0:T(8,128)(2,1)}), bf16[32,80,128]{2,1,0:T(8,128)(2,1)S(1)}, u32[]{:S(2)}, u32[]{:S(2)}) async-start(bf16[32,80,128]{2,1,0:T(8,128)(2,1)} %shard_map.82), calls=%async_computation | async-start | bytes 1310720 | tf_op jit(solution)/shard_map/all_to_all | solution.py:341
  22.1 0.0 copy-done.2
  22.1 0.1 copy.16
  23.5 0.0 copy-done.4
  23.5 0.6 reshape.95.speed_ref
  24.1 0.0 copy-done.3
  24.1 0.7 reshape.93.react_ref
  24.7 0.0 copy-done.5
  24.7 0.1 fusion.15
  24.8 0.1 broadcast_in_dim.40
  24.9 0.1 reshape.92
  25.0 0.1 reshape_squeeze.3
  25.1 0.2 select_reduce_fusion
  25.3 0.2 fusion.1
  25.5 0.6 add_add_fusion.1
  26.1 12.2 %all-to-all-done.faces_ref = bf16[32,80,128]{2,1,0:T(8,128)(2,1)S(1)} async-done(((bf16[32,80,128]{2,1,0:T(8,128)(2,1)}), bf16[32,80,128]{2,1,0:T(8,128)(2,1)S(1)}, u32[]{:S(2)}, u32[]{:S(2)}) %all-to-all-start) | async-done | bytes 655392 | tf_op jit(solution)/shard_map/all_to_all | solution.py:341
  38.3 0.0 copy-start.1
  38.3 0.8 copy-done.1
  39.2 16.8 %shard_map.84 = bf16[1,10,32,1024]{3,2,1,0:T(8,128)(2,1)} custom-call(s32[56]{0:T(128)} %get-tuple-element.9.meta_ref, f32[12]{0:T(128)} %reshape.95.speed_ref, f32[10]{0:T(128)} %rate_ref.3, f32[100]{0:T(128)} %reshape.93.react_ref, bf16[4,10,32,1024]{3,2,1,0:T(8,128)(2,1)} %bitcast.26, bf16[32,80,128]{2,1,0:T(8,128)(2,1)} %copy-done.1), custom_call_target="tpu_custom_call" | custom-call | flops 40000000000 | bytes 1400000 | tf_op jit(solution)/shard_map/pallas_call | solution.py:287
  56.0 1.7 %collective-permute-start = (bf16[1,10,32,1024]{3,2,1,0:T(8,128)(2,1)}, bf16[1,10,32,1024]{3,2,1,0:T(8,128)(2,1)S(1)}, u32[]{:S(2)}, u32[]{:S(2)}) collective-permute-start(bf16[1,10,32,1024]{3,2,1,0:T(8,128)(2,1)} %shard_map.84), channel_id=1, source_target_pairs={{0,16},{16,0},{1,17},{17,1},{2,18},{18,2},{3,19},{19,3},{4,20},{20... | collective-permute-start | bytes 1966088 | tf_op jit(solution)/shard_map/ppermute | solution.py:15
  57.7 0.0 copy-start
  57.7 45.5 %shard_map.83 = bf16[4,10,32,1024]{3,2,1,0:T(8,128)(2,1)} custom-call(s32[56]{0:T(128)} %get-tuple-element.10.meta_ref, f32[12]{0:T(128)} %reshape.95.speed_ref, f32[10]{0:T(128)} %rate_ref.3, f32[100]{0:T(128)} %reshape.93.react_ref, bf16[4,10,32,1024]{3,2,1,0:T(8,128)(2,1)} %bitcast.27, bf16[32,80,128]{2,1,0:T(8,128)(2,1)} %copy-done.1), custom_call_target="tpu_custom_call" | custom-call | flops 120000004096 | bytes 4200000 | tf_op jit(solution)/shard_map/pallas_call | solution.py:287
  103.2 0.0 collective-permute-done
  103.2 0.0 copy-done
  103.2 1.1 %bitcast_dynamic-update-slice_fusion = bf16[1,4,10,32,1024]{4,3,2,1,0:T(8,128)(2,1)} fusion(bf16[1,4,10,32,1024]{4,3,2,1,0:T(8,128)(2,1)} %bitcast.30, s32[]{:T(128)S(6)} %select_n.97, bf16[1,10,32,1024]{3,2,1,0:T(8,128)(2,1)S(1)} %collective-permute-done, bf16[1,10,32,1024]{3,2,1,0:T(8,128)(2,1)S(1)} %copy-done, pred[]{:T(512)} %bitcast.9), kind=kLoop, calls=%fused_computation | loop fusion | flops 327680 | bytes 1966596 | tf_op jit(solution)/shard_map/jit(dynamic_update_index_in_dim)/dynamic_update_slice | solution.py:374
  (11 shorter events, 0.1 us)
Async XLA Ops:
  0.0 22.1 %copy-start.2 = (s32[1,64,6]{1,0,2:T(1,128)S(1)}, s32[1,64,6]{1,0,2:T(1,128)}, u32[]{:S(2)}) copy-start(s32[1,64,6]{1,0,2:T(1,128)} %param.13) | copy-start | bytes 4612
  0.0 23.5 %copy-start.4 = (bf16[1,4,3]{2,1,0:T(4,128)(2,1)S(1)}, bf16[1,4,3]{2,1,0:T(4,128)(2,1)}, u32[]{:S(2)}) copy-start(bf16[1,4,3]{2,1,0:T(4,128)(2,1)} %param.10) | copy-start | bytes 76
  0.0 24.1 %copy-start.3 = (f32[10,10]{1,0:T(8,128)S(1)}, f32[10,10]{1,0:T(8,128)}, u32[]{:S(2)}) copy-start(f32[10,10]{1,0:T(8,128)} %param.12) | copy-start | bytes 1204
  0.0 24.7 %copy-start.5 = (s32[1,64]{1,0:T(1,128)S(1)}, s32[1,64]{1,0:T(1,128)}, u32[]{:S(2)}) copy-start(s32[1,64]{1,0:T(1,128)} %param.9) | copy-start | bytes 772
  15.8 22.5 %all-to-all-start = ((bf16[32,80,128]{2,1,0:T(8,128)(2,1)}), bf16[32,80,128]{2,1,0:T(8,128)(2,1)S(1)}, u32[]{:S(2)}, u32[]{:S(2)}) async-start(bf16[32,80,128]{2,1,0:T(8,128)(2,1)} %shard_map.82), calls=%async_computation | async-start | bytes 1310720 | tf_op jit(solution)/shard_map/all_to_all | solution.py:341
  38.3 0.8 copy-start.1
  56.0 47.2 %collective-permute-start = (bf16[1,10,32,1024]{3,2,1,0:T(8,128)(2,1)}, bf16[1,10,32,1024]{3,2,1,0:T(8,128)(2,1)S(1)}, u32[]{:S(2)}, u32[]{:S(2)}) collective-permute-start(bf16[1,10,32,1024]{3,2,1,0:T(8,128)(2,1)} %shard_map.84), channel_id=1, source_target_pairs={{0,16},{16,0},{1,17},{17,1},{2,18},{18,2},{3,19},{19,3},{4,20},{20... | collective-permute-start | bytes 1966088 | tf_op jit(solution)/shard_map/ppermute | solution.py:15
  57.7 45.5 %copy-start = (bf16[1,10,32,1024]{3,2,1,0:T(8,128)(2,1)S(1)}, bf16[1,10,32,1024]{3,2,1,0:T(8,128)(2,1)}, u32[]{:S(2)}) copy-start(bf16[1,10,32,1024]{3,2,1,0:T(8,128)(2,1)} %shard_map.84) | copy-start | bytes 1966084

commit v3 on v0

--- a/solution.py
+++ b/solution.py
@@ -2,6 +2,7 @@
 
 import jax
 import jax.numpy as jnp
+import numpy as np
 from jax import lax
 from jax.experimental import pallas as pl
 from jax.experimental.pallas import tpu as pltpu
@@ -23,11 +24,44 @@
     return lax.broadcasted_iota(jnp.int32, (8, 128), 0)
 
 
+def ones_where(mask):
+    return jnp.asarray(np.where(mask, 1.0, 0.0), jnp.bfloat16)
+
+
 def regroup_matrix():
-    r = lax.broadcasted_iota(jnp.int32, (512, 512), 0)
-    c = lax.broadcasted_iota(jnp.int32, (512, 512), 1)
-    target = (r // 32) % 4 * 128 + r // 128 * 32 + r % 32
-    return jnp.where(c == target, 1.0, 0.0).astype(jnp.bfloat16)
+    r, c = np.arange(512)[:, None], np.arange(512)[None, :]
+    return ones_where(c == r // 32 % 4 * 128 + r // 128 * 32 + r % 32)
+
+
+def shift_matrix():
+    r, c = np.arange(256)[:, None] % 128, np.arange(256)[None, :]
+    lane = c % 128
+    lower = (c < 128) & (r == lane - 1) & (lane % 32 != 0)
+    upper = (c >= 128) & (r == lane + 1) & (lane % 32 != 31)
+    return ones_where(lower | upper)
+
+
+def end_matrix():
+    r, c = np.arange(512)[:, None], np.arange(1024)[None, :]
+    side, j = r // 128 % 2, r % 32
+    return ones_where((c // 128 + c // 32 % 4 * 8 == j) & (c % 32 == side * 31))
+
+
+def face_matrix_z():
+    r, c = np.arange(1024)[:, None], np.arange(256)[None, :]
+    return ones_where((r // 32 == c % 32) & (r % 32 == c // 128 * 31))
+
+
+def face_matrix_y():
+    r, c = np.arange(256)[:, None], np.arange(256)[None, :]
+    return ones_where((r // 32 == c // 128 * 7) & (r % 32 == c % 32))
+
+
+def coarse_matrices():
+    r, c = np.arange(128)[:, None], np.arange(128)[None, :]
+    pairs = (r // 2 == c // 2) * 0.5
+    patches = (r // 64 == c // 64) * (r % 32 // 2 == c % 32 // 2) * 0.25
+    return jnp.asarray(np.stack([r == c, pairs, patches]).astype(np.float32), jnp.bfloat16)
 
 
 def regroup_in(x_ref, matrix, rows):
@@ -50,51 +84,39 @@
     return pl.ds(jj * fields * 32 + f * 32 + ii, 8, stride=4)
 
 
-def pack_kernel(sel_ref, x_ref, out_ref, faces, rows, matrix):
+def pack_kernel(
+    sel_ref, x_ref, matrix, pick_z, pick_y, out_ref, faces, rows, edges
+):
     step = pl.program_id(0)
     fields = x_ref.shape[1]
-    lane = lane_iota()
-    k = lane % 32
-
-    @pl.when(step == 0)
-    def _():
-        matrix[...] = regroup_matrix()
-
+    height = fields * 32
+    group = lane_iota() // 32
     regroup_in(x_ref, matrix, rows)
-
-    def pair(fp, carry):
+    along_z = jnp.dot(
+        x_ref[0].reshape(height, 1024), pick_z[...], preferred_element_type=jnp.float32
+    )
+    ends = jnp.concatenate([x_ref[0, :, :, :128], x_ref[0, :, :, 896:]], axis=2)
+    along_y = jnp.dot(
+        ends.reshape(height, 256), pick_y[...], preferred_element_type=jnp.float32
+    )
+    for side in range(2):
+        edges[side] = along_y[:, 128 * side : 128 * side + 128]
+        edges[2 + side] = along_z[:, 128 * side : 128 * side + 128]
+
+    for fp in range(fields // 2):
         got = [[], [], [], [], [], []]
-        for half in range(2):
-            f = fp * 2 + half
-            got[0].append(rows[pl.ds(f * 32, 8, stride=fields * 32), :])
-            got[1].append(rows[pl.ds(f * 32 + 31, 8, stride=fields * 32), :])
-            low_y = high_y = low_z = high_z = jnp.zeros((8, 128), jnp.float32)
-            for ii in range(4):
-                for jj in range(8):
-                    plane = rows[plane_rows(fields, f, ii, jj), :]
-                    n = ii * 8 + jj
-                    here = k == n
-                    low_z = jnp.where(here, pltpu.roll(plane, n, 1) if n else plane, low_z)
-                    high_z = jnp.where(
-                        here, pltpu.roll(plane, n + 97, 1) if n != 31 else plane, high_z
-                    )
-                    here = lane // 32 == ii
-                    if jj == 0:
-                        low_y = jnp.where(here, pltpu.roll(plane, 32 * ii, 1) if ii else plane, low_y)
-                    if jj == 7:
-                        moved = pltpu.roll(plane, 32 * ii + 32, 1) if ii != 3 else plane
-                        high_y = jnp.where(here, moved, high_y)
-            got[2].append(low_y)
-            got[3].append(high_y)
-            got[4].append(low_z)
-            got[5].append(high_z)
-        at = pl.multiple_of(fp * 16, 16)
+        for f in (fp * 2, fp * 2 + 1):
+            got[0].append(rows[pl.ds(f * 32, 8, stride=height), :])
+            got[1].append(rows[pl.ds(f * 32 + 31, 8, stride=height), :])
+            for face in range(2, 6):
+                v = edges[face - 2, pl.ds(f * 32, 8, stride=4), :]
+                for ii in range(1, 4):
+                    part = edges[face - 2, pl.ds(f * 32 + ii, 8, stride=4), :]
+                    v = jnp.where(group == ii, part, v)
+                got[face].append(v)
         for face in range(6):
             both = jnp.concatenate(got[face], axis=0).astype(jnp.bfloat16)
-            faces[step * 6 + face, pl.ds(at, 16), :] = both
-        return carry
-
-    lax.fori_loop(0, fields // 2, pair, 0)
+            faces[step * 6 + face, fp * 16 : fp * 16 + 16, :] = both
 
     @pl.when(step == pl.num_programs(0) - 1)
     def _():
@@ -112,31 +134,28 @@
         grid_spec=pltpu.PrefetchScalarGridSpec(
             num_scalar_prefetch=1,
             grid=(per_dev,),
-            in_specs=[pl.BlockSpec((1, fields, cells, plane), lambda g, *_: (g, 0, 0, 0))],
+            in_specs=[
+                pl.BlockSpec((1, fields, cells, plane), lambda g, *_: (g, 0, 0, 0)),
+                pl.BlockSpec((512, 512), lambda g, *_: (0, 0)),
+                pl.BlockSpec((1024, 256), lambda g, *_: (0, 0)),
+                pl.BlockSpec((256, 256), lambda g, *_: (0, 0)),
+            ],
             out_specs=pl.BlockSpec((sel.shape[0], fields * 8, 128), lambda g, *_: (0, 0, 0)),
             scratch_shapes=[
                 pltpu.VMEM((per_dev * 6, fields * 8, 128), jnp.bfloat16),
                 pltpu.VMEM((fields * 256, 128), jnp.float32),
-                pltpu.VMEM((512, 512), jnp.bfloat16),
+                pltpu.VMEM((4, fields * 32, 128), jnp.float32),
             ],
         ),
         out_shape=jax.ShapeDtypeStruct((sel.shape[0], fields * 8, 128), jnp.bfloat16),
         compiler_params=pltpu.CompilerParams(vmem_limit_bytes=VMEM_LIMIT),
-    )(sel, blocks)
-
-
-def pair_sum(x, distance, axis, bit_clear):
-    size = x.shape[axis]
-    other = jnp.where(
-        bit_clear, pltpu.roll(x, size - distance, axis), pltpu.roll(x, distance, axis)
-    )
-    return x + other
+    )(sel, blocks, regroup_matrix(), face_matrix_z(), face_matrix_y())
 
 
 def advance_kernel(
     meta_ref, speed_ref, rate_ref, react_ref,
-    x_ref, faces_ref, o_ref,
-    u, ghost, layers, ends, coef, rows, matrix,
+    x_ref, faces_ref, matrix, shift, spread_ends, coarse, o_ref,
+    u, ghost, layers, ends, coef, rows, end_rows,
 ):
     fields = x_ref.shape[1]
     step = pl.program_id(0)
@@ -149,31 +168,25 @@
     scale = substeps.astype(jnp.float32)
     dt = jnp.where(own_level == 0, dt_base, jnp.where(own_level == 1, dt_base / 2, dt_base / 4))
     lane, row = lane_iota(), row_iota()
-    k = lane % 32
-    at_low_z, at_high_z = k == 0, k == 31
-
-    @pl.when(step == 0)
-    def _():
-        matrix[...] = regroup_matrix()
-
     regroup_in(x_ref, matrix, rows)
 
-    tall_lane = lax.broadcasted_iota(jnp.int32, (fields * 8, 128), 1)
     tall_row = lax.broadcasted_iota(jnp.int32, (fields * 8, 128), 0)
     for face in range(6):
         request = block * 6 + face
-        layers[face] = faces_ref[meta_ref[2 * per_dev + request]].astype(jnp.float32)
-
-        @pl.when(meta_ref[2 * per_dev + requests + request] > 0)
-        def _():
-            v = pair_sum(layers[face], 1, 1, tall_lane % 2 == 0)
-            if face < 2:
-                v = pair_sum(v, 1, 0, tall_row % 2 == 0)
-            elif face < 4:
-                v = pair_sum(v, 32, 1, tall_lane // 32 % 2 == 0)
-            else:
-                v = pair_sum(v, 8, 1, tall_lane // 8 % 2 == 0)
-            layers[face] = v * 0.25
+        flag = meta_ref[2 * per_dev + requests + request]
+        which = flag if face < 2 else flag * 2
+        layer = faces_ref[meta_ref[2 * per_dev + request]]
+        layers[face] = jnp.dot(layer, coarse[which], preferred_element_type=jnp.float32)
+        if face < 2:
+
+            @pl.when(flag > 0)
+            def _():
+                v = layers[face]
+                size = fields * 8
+                other = jnp.where(
+                    tall_row % 2 == 0, pltpu.roll(v, size - 1, 0), pltpu.roll(v, 1, 0)
+                )
+                layers[face] = (v + other) * 0.5
 
     speeds = [speed_ref[block * 3 + d] for d in range(3)]
     minus = [jnp.maximum(v, 0.0) * scale * dt for v in speeds]
@@ -200,8 +213,8 @@
         coef[f, 1] = jnp.full((8, 128), rate + plus[0])
         coef[f, 2] = jnp.full((8, 128), rate + minus[1])
         coef[f, 3] = jnp.full((8, 128), rate + plus[1])
-        coef[f, 4] = jnp.where(at_low_z, 0.0, rate + minus[2])
-        coef[f, 5] = jnp.where(at_high_z, 0.0, rate + plus[2])
+        coef[f, 4] = jnp.full((8, 128), rate + minus[2])
+        coef[f, 5] = jnp.full((8, 128), rate + plus[2])
         for e in range(fields):
             own = jnp.where(f == e, 1.0 - 6.0 * rate - outflow, 0.0)
             coef[f, 6 + e] = jnp.full((8, 128), dt * react_ref[f * fields + e] + own)
@@ -211,14 +224,14 @@
         low_z = layers[4, at, :] * (rate + minus[2])
         high_z = layers[5, at, :] * (rate + plus[2])
         for ii in range(4):
+            here = lane // 32 == ii
+            at = pl.ds(f * 32 + ii * 8, 8)
+            end_rows[0, at, :] = jnp.where(here, low_z, 0.0)
+            end_rows[1, at, :] = jnp.where(here, high_z, 0.0)
             ends[0, f, ii] = pltpu.roll(low_y, 128 - 32 * ii, 1) if ii else low_y
             ends[1, f, ii] = pltpu.roll(high_y, 96 - 32 * ii, 1) if ii != 3 else high_y
         for ii in range(4):
             for jj in range(8):
-                n = ii * 8 + jj
-                low = pltpu.roll(low_z, 128 - n, 1) if n else low_z
-                high = pltpu.roll(high_z, 31 - n, 1) if n != 31 else high_z
-                ghost[f, ii, jj] = jnp.where(at_low_z, low, jnp.where(at_high_z, high, 0.0))
                 plane = rows[plane_rows(fields, f, ii, jj), :]
                 u[0, f, ii + 1, jj + 1] = plane
                 if ii == 0:
@@ -231,7 +244,18 @@
                     u[0, f, ii + 1, 0] = halo_low_y(plane, f, ii)
         return carry
 
-    lax.fori_loop(0, fields, prepare, 0)
+    lax.fori_loop(0, fields, prepare, 0, unroll=2)
+
+    low_high = jnp.concatenate([end_rows[0], end_rows[1]], axis=1)
+    coarse_part = low_high.astype(jnp.bfloat16)
+    fine_part = (low_high - coarse_part.astype(jnp.float32)).astype(jnp.bfloat16)
+    spread = jnp.dot(
+        jnp.concatenate([coarse_part, fine_part], axis=1),
+        spread_ends[...],
+        preferred_element_type=jnp.float32,
+    )
+    for jj in range(8):
+        ghost[jj] = spread[:, 128 * jj : 128 * jj + 128]
 
     def substep(index, carry):
         now = index % 2
@@ -239,18 +263,26 @@
 
         def planes(jj, inner):
             mid = [[u[now, f, ii + 1, jj + 1] for ii in range(4)] for f in range(fields)]
+            value = jnp.concatenate([v for four in mid for v in four], axis=0)
+            high = value.astype(jnp.bfloat16)
+            low = (value - high.astype(jnp.float32)).astype(jnp.bfloat16)
+            along_z = jnp.dot(
+                jnp.concatenate([high, low], axis=1),
+                shift[...],
+                preferred_element_type=jnp.float32,
+            )
             for f in range(fields):
                 before = [u[now, f, 0, jj + 1]] + mid[f][:-1]
                 after = mid[f][1:] + [u[now, f, 5, jj + 1]]
                 total = []
                 for ii in range(4):
-                    c = mid[f][ii]
-                    v = ghost[f, ii, jj] + coef[f, 0] * before[ii]
+                    at = f * 32 + ii * 8
+                    v = ghost[jj, at : at + 8, :] + coef[f, 0] * before[ii]
                     v = v + coef[f, 1] * after[ii]
                     v = v + coef[f, 2] * u[now, f, ii + 1, jj]
                     v = v + coef[f, 3] * u[now, f, ii + 1, jj + 2]
-                    v = v + coef[f, 4] * pltpu.roll(c, 1, 1)
-                    v = v + coef[f, 5] * pltpu.roll(c, 127, 1)
+                    v = v + coef[f, 4] * along_z[at : at + 8, :128]
+                    v = v + coef[f, 5] * along_z[at : at + 8, 128:]
                     total.append(v)
                 for e in range(fields):
                     weight = coef[f, 6 + e]
@@ -311,18 +343,22 @@
             in_specs=[
                 pl.BlockSpec(block_shape, picked),
                 pl.BlockSpec(faces.shape, lambda g, *_: (0, 0, 0)),
+                pl.BlockSpec((512, 512), lambda g, *_: (0, 0)),
+                pl.BlockSpec((256, 256), lambda g, *_: (0, 0)),
+                pl.BlockSpec((512, 1024), lambda g, *_: (0, 0)),
+                pl.BlockSpec((3, 128, 128), lambda g, *_: (0, 0, 0)),
             ],
             out_specs=pl.BlockSpec(
                 block_shape, picked if out_blocks > 1 else lambda g, *_: (0, 0, 0, 0)
             ),
             scratch_shapes=[
                 pltpu.VMEM((2, fields, 6, 10, 8, 128), jnp.float32),
-                pltpu.VMEM((fields, 4, 8, 8, 128), jnp.float32),
+                pltpu.VMEM((8, fields * 32, 128), jnp.float32),
                 pltpu.VMEM((6, fields * 8, 128), jnp.float32),
                 pltpu.VMEM((2, fields, 4, 8, 128), jnp.float32),
                 pltpu.VMEM((fields, 6 + fields, 8, 128), jnp.float32),
                 pltpu.VMEM((fields * 256, 128), jnp.float32),
-                pltpu.VMEM((512, 512), jnp.bfloat16),
+                pltpu.VMEM((2, fields * 32, 128), jnp.float32),
             ],
         ),
         out_shape=jax.ShapeDtypeStruct((out_blocks, fields, cells, plane), jnp.bfloat16),
@@ -330,7 +366,10 @@
         cost_estimate=pl.CostEstimate(
             flops=count * 40_000_000_000, bytes_accessed=count * 1_400_000, transcendentals=0
         ),
-    )(meta, *scalars, blocks, faces)
+    )(
+        meta, *scalars, blocks, faces,
+        regroup_matrix(), shift_matrix(), end_matrix(), coarse_matrices(),
+    )
 
 
 def local(

time: 98.2 us -> 107 us (1.090)
  the two profiles are of different devices: /device:TPU:1 before, /device:TPU:8 now
where the time goes in v3:
time: 107 us; the launch traced here: 106 us
  Pallas kernels  77.4 us (72%)
  waiting for transfers between devices  12.2 us (11%)
  starting transfers between devices  7.78 us (7%)
  other arithmetic  3.75 us (4%)
  local copies, waits for them, and re-layouts  3.04 us (3%)
  between operations  1.41 us (1%)
    pallas_call x2, Pallas kernels, advance(): pl.pallas_call(advance_kernel, grid_spec=pltpu.PrefetchScalarGridSpec(num...  70.7 us
    all_to_all x1, waiting for transfers between devices, local(): lax.all_to_all(outgoing, ('gy', 'gz'), split_axis=0, concat_axis=0, tiled...  12.2 us
    pallas_call x1, Pallas kernels, pack_faces(): pl.pallas_call(pack_kernel, grid_spec=pltpu.PrefetchScalarGridSpec(num_sc...  6.68 us
    all_to_all x1, starting transfers between devices, local(): lax.all_to_all(outgoing, ('gy', 'gz'), split_axis=0, concat_axis=0, tiled...  6.27 us
  transfers between devices with their start and end apart: 2, of which 1 were waited for; matrix products, arithmetic and copies ran while one was open for 3% of the time, Pallas kernels for 49%

profile of v3, /device:TPU:8, one launch (start us, length us, event | category | flops | bytes accessed | tf_op | source)
XLA Modules:
  0.0 105.6 jit_solution(66893143207895226)
XLA Ops:
  0.0 0.1 add.98
  0.1 0.1 add.93
  0.2 0.7 select_reduce_fusion.2
  1.0 0.1 reduce_min.14
  1.0 0.1 reduce_max.14
  1.1 0.1 reduce_min.18
  1.3 0.1 reduce_max.18
  1.4 0.1 copy.32
  1.5 0.1 reshape.94
  1.6 0.6 and_select_fusion.sel_ref
  2.2 0.0 copy-start.2
  2.2 0.0 copy-start.4
  2.2 0.0 copy-start.3
  2.2 0.0 copy-start.5
  2.2 6.7 %shard_map.181 = bf16[32,80,128]{2,1,0:T(8,128)(2,1)} custom-call(s32[32]{0:T(128)} %and_select_fusion.sel_ref, bf16[4,10,32,1024]{3,2,1,0:T(8,128)(2,1)} %bitcast.25, bf16[512,512]{1,0:T(8,128)(2,1)} %constant.117.clone.matrix, bf16[1024,256]{1,0:T(8,128)(2,1)} %constant.118.clone.pick_z, bf16[256,256]{1,0:T(8,128)(2,1)} %constant.119.clone.pick_y), custom_call_target="tpu_custom_call" | custom-call | tf_op jit(solution)/shard_map/pallas_call | solution.py:132
  8.9 6.3 %all-to-all-start = ((bf16[32,80,128]{2,1,0:T(8,128)(2,1)}), bf16[32,80,128]{2,1,0:T(8,128)(2,1)S(1)}, u32[]{:S(2)}, u32[]{:S(2)}) async-start(bf16[32,80,128]{2,1,0:T(8,128)(2,1)} %shard_map.181), calls=%async_computation | async-start | bytes 1310720 | tf_op jit(solution)/shard_map/all_to_all | solution.py:400
  15.1 0.0 copy-done.2
  15.1 0.1 copy.27
  16.5 0.0 copy-done.4
  16.5 0.6 reshape.95.speed_ref
  17.2 0.0 copy-done.3
  17.2 0.7 reshape.93.react_ref
  17.8 0.0 copy-done.5
  17.8 0.1 fusion.15
  17.9 0.1 broadcast_in_dim.40
  18.0 0.1 reshape.92
  18.0 0.1 reshape_squeeze.3
  18.2 0.2 select_reduce_fusion
  18.4 0.2 fusion.1
  18.6 0.6 add_add_fusion.1
  19.2 12.2 %all-to-all-done.faces_ref = bf16[32,80,128]{2,1,0:T(8,128)(2,1)S(1)} async-done(((bf16[32,80,128]{2,1,0:T(8,128)(2,1)}), bf16[32,80,128]{2,1,0:T(8,128)(2,1)S(1)}, u32[]{:S(2)}, u32[]{:S(2)}) %all-to-all-start) | async-done | bytes 655392 | tf_op jit(solution)/shard_map/all_to_all | solution.py:400
  31.4 0.0 copy-start.1
  31.4 0.8 copy-done.1
  32.2 19.3 %shard_map.183 = bf16[1,10,32,1024]{3,2,1,0:T(8,128)(2,1)} custom-call(s32[56]{0:T(128)} %get-tuple-element.9.meta_ref, f32[12]{0:T(128)} %reshape.95.speed_ref, f32[10]{0:T(128)} %rate_ref.3, f32[100]{0:T(128)} %reshape.93.react_ref, bf16[4,10,32,1024]{3,2,1,0:T(8,128)(2,1)} %bitcast.26, bf16[32,80,128]{2,1,0:T(8,128)(2,1)} %copy-done.1, ...), custom_call_target="tpu_custom_call" | custom-call | flops 40000000000 | bytes 1400000 | tf_op jit(solution)/shard_map/pallas_call | solution.py:338
  51.5 1.5 %collective-permute-start = (bf16[1,10,32,1024]{3,2,1,0:T(8,128)(2,1)}, bf16[1,10,32,1024]{3,2,1,0:T(8,128)(2,1)S(1)}, u32[]{:S(2)}, u32[]{:S(2)}) collective-permute-start(bf16[1,10,32,1024]{3,2,1,0:T(8,128)(2,1)} %shard_map.183), channel_id=1, source_target_pairs={{0,16},{16,0},{1,17},{17,1},{2,18},{18,2},{3,19},{19,3},{4,20},{20... | collective-permute-start | bytes 1966088 | tf_op jit(solution)/shard_map/ppermute | solution.py:16
  53.0 0.0 copy-start
  53.0 51.4 %shard_map.182 = bf16[4,10,32,1024]{3,2,1,0:T(8,128)(2,1)} custom-call(s32[56]{0:T(128)} %get-tuple-element.10.meta_ref, f32[12]{0:T(128)} %reshape.95.speed_ref, f32[10]{0:T(128)} %rate_ref.3, f32[100]{0:T(128)} %reshape.93.react_ref, bf16[4,10,32,1024]{3,2,1,0:T(8,128)(2,1)} %bitcast.27, bf16[32,80,128]{2,1,0:T(8,128)(2,1)} %copy-done.1, ...), custom_call_target="tpu_custom_call" | custom-call | flops 120000004096 | bytes 4200000 | tf_op jit(solution)/shard_map/pallas_call | solution.py:338
  104.5 0.0 collective-permute-done
  104.5 0.0 copy-done
  104.5 1.1 %bitcast_dynamic-update-slice_fusion = bf16[1,4,10,32,1024]{4,3,2,1,0:T(8,128)(2,1)} fusion(bf16[1,4,10,32,1024]{4,3,2,1,0:T(8,128)(2,1)} %bitcast.30, s32[]{:T(128)S(6)} %select_n.97, bf16[1,10,32,1024]{3,2,1,0:T(8,128)(2,1)S(1)} %collective-permute-done, bf16[1,10,32,1024]{3,2,1,0:T(8,128)(2,1)S(1)} %copy-done, pred[]{:T(512)} %bitcast.9), kind=kLoop, calls=%fused_computation | loop fusion | flops 327680 | bytes 1966596 | tf_op jit(solution)/shard_map/jit(dynamic_update_index_in_dim)/dynamic_update_slice | solution.py:433
  (11 shorter events, 0.1 us)
Async XLA Ops:
  2.2 13.0 %copy-start.2 = (s32[1,64,6]{1,0,2:T(1,128)S(1)}, s32[1,64,6]{1,0,2:T(1,128)}, u32[]{:S(2)}) copy-start(s32[1,64,6]{1,0,2:T(1,128)} %param.24) | copy-start | bytes 4612
  2.2 14.4 %copy-start.4 = (bf16[1,4,3]{2,1,0:T(4,128)(2,1)S(1)}, bf16[1,4,3]{2,1,0:T(4,128)(2,1)}, u32[]{:S(2)}) copy-start(bf16[1,4,3]{2,1,0:T(4,128)(2,1)} %param.21) | copy-start | bytes 76
  2.2 15.0 %copy-start.3 = (f32[10,10]{1,0:T(8,128)S(1)}, f32[10,10]{1,0:T(8,128)}, u32[]{:S(2)}) copy-start(f32[10,10]{1,0:T(8,128)} %param.23) | copy-start | bytes 1204
  2.2 15.6 %copy-start.5 = (s32[1,64]{1,0:T(1,128)S(1)}, s32[1,64]{1,0:T(1,128)}, u32[]{:S(2)}) copy-start(s32[1,64]{1,0:T(1,128)} %param.20) | copy-start | bytes 772
  8.9 22.5 %all-to-all-start = ((bf16[32,80,128]{2,1,0:T(8,128)(2,1)}), bf16[32,80,128]{2,1,0:T(8,128)(2,1)S(1)}, u32[]{:S(2)}, u32[]{:S(2)}) async-start(bf16[32,80,128]{2,1,0:T(8,128)(2,1)} %shard_map.181), calls=%async_computation | async-start | bytes 1310720 | tf_op jit(solution)/shard_map/all_to_all | solution.py:400
  31.4 0.8 copy-start.1
  51.5 52.9 %collective-permute-start = (bf16[1,10,32,1024]{3,2,1,0:T(8,128)(2,1)}, bf16[1,10,32,1024]{3,2,1,0:T(8,128)(2,1)S(1)}, u32[]{:S(2)}, u32[]{:S(2)}) collective-permute-start(bf16[1,10,32,1024]{3,2,1,0:T(8,128)(2,1)} %shard_map.183), channel_id=1, source_target_pairs={{0,16},{16,0},{1,17},{17,1},{2,18},{18,2},{3,19},{19,3},{4,20},{20... | collective-permute-start | bytes 1966088 | tf_op jit(solution)/shard_map/ppermute | solution.py:16
  53.0 51.4 %copy-start = (bf16[1,10,32,1024]{3,2,1,0:T(8,128)(2,1)S(1)}, bf16[1,10,32,1024]{3,2,1,0:T(8,128)(2,1)}, u32[]{:S(2)}) copy-start(bf16[1,10,32,1024]{3,2,1,0:T(8,128)(2,1)} %shard_map.183) | copy-start | bytes 1966084
